TPU v7x, 128 devices: a whole 4x4x4 slice. The times are simulated.
128 devices in a mesh: section: 4 (over z), tp: 32 (over x, y, core).
Axes of the slice: x: 4, y: 4, z: 4, core: 2. Of those that a mesh axis runs over, the one named last changes fastest.
Arguments:
- entering: bfloat16 [2, 88, 16384], P(None, None, 'tp'), may hold values from -6 to 6
- norm_gain: bfloat16 [4, 16384], P('section', 'tp'), may hold values from 0.099609375 to 1.8984375
- query_weight: bfloat16 [4, 16384, 8192], P(None, ('section', 'tp')), may hold values from -0.046875 to 0.046875
- key_matrix: bfloat16 [4, 16384, 512], P(None, ('section', 'tp')), may hold values from -0.046875 to 0.046875
- value_matrix: bfloat16 [4, 16384, 512], P(None, ('section', 'tp')), may hold values from -0.046875 to 0.046875
- output_weight: bfloat16 [4, 8192, 16384], P(None, ('section', 'tp')), may hold values from -0.0625 to 0.0625
Outputs:
- section_outputs: bfloat16 [4, 2, 88, 16384], P('section', None, None, 'tp')
All inputs are finite; a program needn't handle non-finite values.
Results may differ from a plain program's by a relative error of at most 0.017.
Values may be sent and summed in bfloat16 or wider, within the bound.
No kernel may reach another device: no remote copies, remote signals or barrier semaphores. Data moves between devices by JAX's collectives and lax.ppermute only.
A program may use at most 128 MiB of HBM per device.

v0:
```python
import math

import jax
import jax.numpy as jnp
from jax import lax
from jax.sharding import PartitionSpec as P

QUERY_HEAD_COUNT = 64
KEY_VALUE_HEADS = 4
HEAD_SIZE = 128


def shifted(value, axis, by):
    count = lax.axis_size(axis)
    pairs = [(i, i + by) for i in range(count) if 0 <= i + by < count]
    return lax.ppermute(value, axis, pairs)


def split_columns(weights, parts):
    count, height, width = weights.shape
    return weights.reshape(count, height, parts, width // parts).transpose(0, 2, 1, 3)


def split_strided(weights, parts):
    count, height, width = weights.shape
    return weights.reshape(count, height, width // parts, parts).transpose(0, 3, 1, 2)


def body(entering, norm_gain, query_weight, key_matrix, value_matrix, output_weight):
    section_count = lax.axis_size("section")
    column_count = lax.axis_size("tp")
    query_parts = split_columns(query_weight, column_count)
    key_parts = split_strided(key_matrix, column_count)
    value_parts = split_strided(value_matrix, column_count)
    output_parts = split_columns(output_weight, column_count)
    flat_count = section_count * column_count
    relayed = (
        lax.all_to_all(
            query_parts.reshape(flat_count, query_parts.shape[2], query_parts.shape[3]),
            ("section", "tp"),
            split_axis=0,
            concat_axis=0,
            tiled=True,
        ),
        lax.all_to_all(
            key_parts.reshape(flat_count, key_parts.shape[2], key_parts.shape[3]),
            ("section", "tp"),
            split_axis=0,
            concat_axis=0,
            tiled=True,
        ),
        lax.all_to_all(
            value_parts.reshape(flat_count, value_parts.shape[2], value_parts.shape[3]),
            ("section", "tp"),
            split_axis=0,
            concat_axis=0,
            tiled=True,
        ),
        lax.all_to_all(
            output_parts.reshape(flat_count, output_parts.shape[2], output_parts.shape[3]),
            ("section", "tp"),
            split_axis=0,
            concat_axis=0,
            tiled=True,
        ),
    )
    local_query = relayed[0].reshape(-1, relayed[0].shape[-1])
    local_key = relayed[1].reshape(-1, relayed[1].shape[-1])
    local_value = relayed[2].reshape(-1, relayed[2].shape[-1])
    local_output = relayed[3].reshape(-1, relayed[3].shape[-1])
    section_index = lax.axis_index("section")
    column_index = lax.axis_index("tp")
    heads_here = local_query.shape[1] // HEAD_SIZE
    query_group_width = QUERY_HEAD_COUNT // KEY_VALUE_HEADS
    own_head = column_index * heads_here // query_group_width
    kv_width = local_key.shape[1]
    scale_factor = 1.0 / math.sqrt(HEAD_SIZE)
    batch_count = entering.shape[0]
    incoming = jnp.zeros_like(entering[0])
    records = [jnp.zeros_like(entering[0]) for batch_index in range(batch_count)]
    tick_count = batch_count + section_count - 1
    for moment in range(tick_count):
        if moment < batch_count:
            source = jnp.where(section_index == 0, entering[moment], incoming)
        else:
            source = incoming
        local_token_count = source.shape[0]
        whole = lax.all_gather(source, "tp", axis=1, tiled=True)
        gain_whole = lax.all_gather(norm_gain, "tp", axis=1, tiled=True)
        widened = whole.astype(jnp.float32)
        normed = (
            widened
            * lax.rsqrt(jnp.mean(widened * widened, axis=-1, keepdims=True) + 1e-05)
            * gain_whole.astype(jnp.float32)
        ).astype(jnp.bfloat16)
        query_rows = jnp.dot(normed, local_query, preferred_element_type=jnp.float32).astype(
            jnp.bfloat16
        )
        kv_piece = jnp.concatenate(
            [
                jnp.dot(normed, local_key, preferred_element_type=jnp.float32),
                jnp.dot(normed, local_value, preferred_element_type=jnp.float32),
            ],
            axis=1,
        ).astype(jnp.bfloat16)
        kv_whole = lax.all_gather(kv_piece, "tp", axis=1, tiled=True)
        kv_split = kv_whole.reshape(local_token_count, column_count, 2, kv_width)
        key_row_block = (
            kv_split[:, :, 0, :]
            .transpose(0, 2, 1)
            .reshape(local_token_count, column_count * kv_width)
        )
        value_row_block = (
            kv_split[:, :, 1, :]
            .transpose(0, 2, 1)
            .reshape(local_token_count, column_count * kv_width)
        )
        head_key = lax.dynamic_slice_in_dim(key_row_block, own_head * HEAD_SIZE, HEAD_SIZE, 1)
        head_value = lax.dynamic_slice_in_dim(value_row_block, own_head * HEAD_SIZE, HEAD_SIZE, 1)
        query_heads = query_rows.reshape(local_token_count, heads_here, HEAD_SIZE)
        scores = (
            jnp.einsum("shd,td->hst", query_heads, head_key, preferred_element_type=jnp.float32)
            * scale_factor
        )
        causal = lax.broadcasted_iota(
            jnp.int32, (local_token_count, local_token_count), 0
        ) >= lax.broadcasted_iota(jnp.int32, (local_token_count, local_token_count), 1)
        weights = jnp.where(causal[None], jnp.exp(scores), 0.0)
        shares = (weights / jnp.sum(weights, axis=-1, keepdims=True)).astype(jnp.bfloat16)
        head_mixed = jnp.einsum(
            "hst,td->shd", shares, head_value, preferred_element_type=jnp.float32
        )
        head_mixed = head_mixed.astype(jnp.bfloat16).reshape(
            local_token_count, heads_here * HEAD_SIZE
        )
        residual = source.astype(jnp.float32)
        summed = residual + jnp.dot(
            lax.all_gather(head_mixed, "tp", axis=1, tiled=True),
            local_output,
            preferred_element_type=jnp.float32,
        )
        result = summed.astype(jnp.bfloat16)
        for batch_index in range(batch_count):
            records[batch_index] = jnp.where(
                section_index + batch_index == moment, result, records[batch_index]
            )
        if moment + 1 < tick_count:
            incoming = shifted(result, "section", 1)
    return jnp.stack(records)[None]


def solution(mesh):
    placed = (
        P(None, None, "tp"),
        P("section", "tp"),
        P(None, ("section", "tp"), None),
        P(None, ("section", "tp"), None),
        P(None, ("section", "tp"), None),
        P(None, ("section", "tp"), None),
    )
    return jax.shard_map(
        body, mesh=mesh, in_specs=placed, out_specs=P("section", None, None, "tp"), check_vma=False
    )
```

profile of v0, /device:TPU:5, one launch (start us, length us, event | category | flops | bytes accessed | tf_op | source)
XLA Modules:
  0.0 941.1 jit_solution(12998729675733773766)
XLA Ops:
  8.9 10.8 %all-to-all-start.1 = ((bf16[128,128,16]{1,2,0:T(8,128)(2,1)}), bf16[128,128,16]{1,2,0:T(8,128)(2,1)S(1)}, u32[]{:S(2)}, u32[]{:S(2)}) async-start(bf16[128,128,16]{1,2,0:T(8,128)(2,1)} %bitcast.10), calls=%async_computation.1 | async-start | bytes 1048576 | tf_op jit(solution)/shard_map/all_to_all | solution.py:52
  22.0 9.5 %all-to-all-done.1 = bf16[128,128,16]{1,2,0:T(8,128)(2,1)S(1)} async-done(((bf16[128,128,16]{1,2,0:T(8,128)(2,1)}), bf16[128,128,16]{1,2,0:T(8,128)(2,1)S(1)}, u32[]{:S(2)}, u32[]{:S(2)}) %all-to-all-start.1) | async-done | bytes 524320 | tf_op jit(solution)/shard_map/all_to_all | solution.py:52
  37.8 12.0 %copy.76 = bf16[4,128,8192]{1,2,0:T(8,128)(2,1)} copy(bf16[4,128,8192]{2,1,0:T(8,128)(2,1)} %param.8) | data formatting | bytes 16777216 | tf_op args[2]
  49.7 12.0 %copy.77 = bf16[4,32,128,256]{3,2,1,0:T(8,128)(2,1)} copy(bf16[4,32,128,256]{2,3,1,0:T(8,128)(2,1)} %bitcast.318) | data formatting | bytes 16777216 | tf_op jit(solution)/shard_map/transpose | solution.py:21
  61.7 10.3 %all-to-all-start.2 = ((bf16[128,128,256]{2,1,0:T(8,128)(2,1)}), bf16[128,128,256]{2,1,0:T(8,128)(2,1)}, u32[]{:S(2)}, u32[]{:S(2)}) async-start(bf16[128,128,256]{2,1,0:T(8,128)(2,1)} %bitcast.317), calls=%async_computation.2 | async-start | bytes 16777216 | tf_op jit(solution)/shard_map/all_to_all | solution.py:38
  73.2 10.5 %copy.147 = bf16[32,8,32,512]{3,2,1,0:T(8,128)(2,1)} copy(bf16[32,8,32,512]{3,1,2,0:T(8,128)(2,1)} %bitcast.320) | data formatting | bytes 16777216
  83.7 8.3 bitcast_bitcast_fusion
  92.0 11.5 %copy.81 = bf16[4,32,64,512]{3,2,1,0:T(8,128)(2,1)} copy(bf16[4,32,64,512]{3,1,2,0:T(8,128)(2,1)} %bitcast_bitcast_fusion) | data formatting | bytes 16777216 | tf_op jit(solution)/shard_map/transpose | solution.py:21
  103.5 73.6 %all-to-all-done.2 = bf16[128,128,256]{2,1,0:T(8,128)(2,1)} async-done(((bf16[128,128,256]{2,1,0:T(8,128)(2,1)}), bf16[128,128,256]{2,1,0:T(8,128)(2,1)}, u32[]{:S(2)}, u32[]{:S(2)}) %all-to-all-start.2) | async-done | bytes 8388640 | tf_op jit(solution)/shard_map/all_to_all | solution.py:38
  185.5 114.3 %all_gather.53 = bf16[1,16384]{1,0:T(2,128)(2,1)S(1)} all-gather(bf16[1,512]{1,0:T(2,128)(2,1)S(1)} %copy-done.14), channel_id=1, replica_groups=mesh['section'=4,'tp'=32] {'tp'}, dimensions={1}, use_global_device_ids=true | all-gather | bytes 33792 | tf_op jit(solution)/shard_map/all_gather | solution.py:89
  306.3 22.1 %all_gather.54 = bf16[88,1024]{0,1:T(8,128)(2,1)S(1)} all-gather(bf16[88,32]{0,1:T(8,128)(2,1)S(1)} %pad_maximum_fusion), channel_id=1, replica_groups=mesh['section'=4,'tp'=32] {'tp'}, dimensions={1}, use_global_device_ids=true | all-gather | bytes 185856 | tf_op jit(solution)/shard_map/all_gather | solution.py:106
  334.6 43.5 %all-gather.12.cloned.1.call-done = bf16[88,8192]{1,0:T(8,128)(2,1)} async-done(((bf16[88,256]{1,0:T(8,128)(2,1)}), bf16[88,8192]{1,0:T(8,128)(2,1)}) %all-gather.12.cloned.1.call-update) | async-done | bytes 1441808 | tf_op jit(solution)/shard_map/all_gather | solution.py:138
  389.0 47.5 %all-gather.14.cloned.1.call-done = bf16[88,16384]{1,0:T(8,128)(2,1)} async-done(((bf16[88,512]{1,0:T(8,128)(2,1)}), bf16[88,16384]{1,0:T(8,128)(2,1)}) %all-gather.14.cloned.1.call-update) | async-done | bytes 2883600 | tf_op jit(solution)/shard_map/all_gather | solution.py:88
  443.0 24.3 %all_gather.57 = bf16[88,1024]{0,1:T(8,128)(2,1)S(1)} all-gather(bf16[88,32]{0,1:T(8,128)(2,1)S(1)} %pad_maximum_fusion.1), channel_id=1, replica_groups=mesh['section'=4,'tp'=32] {'tp'}, dimensions={1}, use_global_device_ids=true | all-gather | bytes 185856 | tf_op jit(solution)/shard_map/all_gather | solution.py:106
  473.5 42.0 %all-gather.16.cloned.1.call-done = bf16[88,8192]{1,0:T(8,128)(2,1)} async-done(((bf16[88,256]{1,0:T(8,128)(2,1)}), bf16[88,8192]{1,0:T(8,128)(2,1)}) %all-gather.16.cloned.1.call-update) | async-done | bytes 1441808 | tf_op jit(solution)/shard_map/all_gather | solution.py:138
  526.5 47.6 %all-gather.18.cloned.1.call-done = bf16[88,16384]{1,0:T(8,128)(2,1)} async-done(((bf16[88,512]{1,0:T(8,128)(2,1)}), bf16[88,16384]{1,0:T(8,128)(2,1)}) %all-gather.18.cloned.1.call-update) | async-done | bytes 2883600 | tf_op jit(solution)/shard_map/all_gather | solution.py:88
  580.4 24.1 %all_gather.60 = bf16[88,1024]{0,1:T(8,128)(2,1)S(1)} all-gather(bf16[88,32]{0,1:T(8,128)(2,1)S(1)} %pad_maximum_fusion.2), channel_id=1, replica_groups=mesh['section'=4,'tp'=32] {'tp'}, dimensions={1}, use_global_device_ids=true | all-gather | bytes 185856 | tf_op jit(solution)/shard_map/all_gather | solution.py:106
  610.8 42.0 %all-gather.20.cloned.1.call-done = bf16[88,8192]{1,0:T(8,128)(2,1)} async-done(((bf16[88,256]{1,0:T(8,128)(2,1)}), bf16[88,8192]{1,0:T(8,128)(2,1)}) %all-gather.20.cloned.1.call-update) | async-done | bytes 1441808 | tf_op jit(solution)/shard_map/all_gather | solution.py:138
  664.0 47.3 %all-gather.22.cloned.1.call-done = bf16[88,16384]{1,0:T(8,128)(2,1)} async-done(((bf16[88,512]{1,0:T(8,128)(2,1)}), bf16[88,16384]{1,0:T(8,128)(2,1)}) %all-gather.22.cloned.1.call-update) | async-done | bytes 2883600 | tf_op jit(solution)/shard_map/all_gather | solution.py:88
  717.7 24.1 %all_gather.63 = bf16[88,1024]{0,1:T(8,128)(2,1)S(1)} all-gather(bf16[88,32]{0,1:T(8,128)(2,1)S(1)} %pad_maximum_fusion.3), channel_id=1, replica_groups=mesh['section'=4,'tp'=32] {'tp'}, dimensions={1}, use_global_device_ids=true | all-gather | bytes 185856 | tf_op jit(solution)/shard_map/all_gather | solution.py:106
  748.1 42.0 %all-gather.24.cloned.1.call-done = bf16[88,8192]{1,0:T(8,128)(2,1)} async-done(((bf16[88,256]{1,0:T(8,128)(2,1)}), bf16[88,8192]{1,0:T(8,128)(2,1)}) %all-gather.24.cloned.1.call-update) | async-done | bytes 1441808 | tf_op jit(solution)/shard_map/all_gather | solution.py:138
  801.0 47.5 %all-gather.26.cloned.1.call-done = bf16[88,16384]{1,0:T(8,128)(2,1)} async-done(((bf16[88,512]{1,0:T(8,128)(2,1)}), bf16[88,16384]{1,0:T(8,128)(2,1)}) %all-gather.26.cloned.1.call-update) | async-done | bytes 2883600 | tf_op jit(solution)/shard_map/all_gather | solution.py:88
  855.0 24.4 %all_gather.66 = bf16[88,1024]{0,1:T(8,128)(2,1)S(1)} all-gather(bf16[88,32]{0,1:T(8,128)(2,1)S(1)} %pad_maximum_fusion.4), channel_id=1, replica_groups=mesh['section'=4,'tp'=32] {'tp'}, dimensions={1}, use_global_device_ids=true | all-gather | bytes 185856 | tf_op jit(solution)/shard_map/all_gather | solution.py:106
  885.6 42.1 %all-gather.28.cloned.1.call-done = bf16[88,8192]{1,0:T(8,128)(2,1)} async-done(((bf16[88,256]{1,0:T(8,128)(2,1)}), bf16[88,8192]{1,0:T(8,128)(2,1)}) %all-gather.28.cloned.1.call-update) | async-done | bytes 1441808 | tf_op jit(solution)/shard_map/all_gather | solution.py:138
  (137 shorter events, 133.1 us)
Async XLA Ops:
  8.9 22.7 %all-to-all-start.1 = ((bf16[128,128,16]{1,2,0:T(8,128)(2,1)}), bf16[128,128,16]{1,2,0:T(8,128)(2,1)S(1)}, u32[]{:S(2)}, u32[]{:S(2)}) async-start(bf16[128,128,16]{1,2,0:T(8,128)(2,1)} %bitcast.10), calls=%async_computation.1 | async-start | bytes 1048576 | tf_op jit(solution)/shard_map/all_to_all | solution.py:52
  31.5 30.2 %all-to-all-start = ((bf16[128,128,16]{1,2,0:T(8,128)(2,1)}), bf16[128,128,16]{1,2,0:T(8,128)(2,1)S(1)}, u32[]{:S(2)}, u32[]{:S(2)}) async-start(bf16[128,128,16]{1,2,0:T(8,128)(2,1)} %bitcast.7), calls=%async_computation | async-start | bytes 1048576 | tf_op jit(solution)/shard_map/all_to_all | solution.py:45
  61.7 10.8 %copy-start.13 = (bf16[2,88,512]{2,1,0:T(8,128)(2,1)S(1)}, bf16[2,88,512]{2,1,0:T(8,128)(2,1)}, u32[]{:S(2)}) copy-start(bf16[2,88,512]{2,1,0:T(8,128)(2,1)} %param.6) | copy-start | bytes 540676
  61.7 115.4 %all-to-all-start.2 = ((bf16[128,128,256]{2,1,0:T(8,128)(2,1)}), bf16[128,128,256]{2,1,0:T(8,128)(2,1)}, u32[]{:S(2)}, u32[]{:S(2)}) async-start(bf16[128,128,256]{2,1,0:T(8,128)(2,1)} %bitcast.317), calls=%async_computation.2 | async-start | bytes 16777216 | tf_op jit(solution)/shard_map/all_to_all | solution.py:38
  72.0 227.9 %all-gather.30.cloned.1.call-start = ((), (), s32[]{:S(2)}) async-start(), calls=%async_computation.13 | async-start | bytes 2973696 | tf_op jit(solution)/shard_map/all_gather | solution.py:88
  177.1 157.4 %all-to-all-start.3 = ((bf16[128,64,512]{2,1,0:T(8,128)(2,1)}), bf16[128,64,512]{2,1,0:T(8,128)(2,1)}, u32[]{:S(2)}, u32[]{:S(2)}) async-start(bf16[128,64,512]{2,1,0:T(8,128)(2,1)} %bitcast.316), calls=%async_computation.3 | async-start | bytes 16777216 | tf_op jit(solution)/shard_map/all_to_all | solution.py:59
  185.4 192.7 %all-gather.12.cloned.1.call-start = ((), (), s32[]{:S(2)}) async-start(), calls=%async_computation.4 | async-start | bytes 1486848 | tf_op jit(solution)/shard_map/all_gather | solution.py:138
  328.5 49.6 %copy-start.5 = (bf16[1,88,512]{2,1,0:T(8,128)(2,1)S(1)}, bf16[1,88,512]{2,1,0:T(8,128)(2,1)}, u32[]{:S(2)}) copy-start(bf16[1,88,512]{2,1,0:T(8,128)(2,1)} %slice_select_fusion) | copy-start | bytes 270340
  334.5 102.0 %all-gather.14.cloned.1.call-start = ((), (), s32[]{:S(2)}) async-start(), calls=%async_computation.5 | async-start | bytes 2973696 | tf_op jit(solution)/shard_map/all_gather | solution.py:88
  383.4 4.9 collective-permute-start
  389.0 126.6 %all-gather.16.cloned.1.call-start = ((), (), s32[]{:S(2)}) async-start(), calls=%async_computation.6 | async-start | bytes 1486848 | tf_op jit(solution)/shard_map/all_gather | solution.py:138
  467.4 48.2 %copy-start.6 = (bf16[88,512]{1,0:T(8,128)(2,1)S(1)}, bf16[88,512]{1,0:T(8,128)(2,1)}, u32[]{:S(2)}) copy-start(bf16[88,512]{1,0:T(8,128)(2,1)} %bitcast_select_fusion) | copy-start | bytes 270340
  473.5 100.6 %all-gather.18.cloned.1.call-start = ((), (), s32[]{:S(2)}) async-start(), calls=%async_computation.7 | async-start | bytes 2973696 | tf_op jit(solution)/shard_map/all_gather | solution.py:88
  520.8 4.9 collective-permute-start.1
  526.4 126.4 %all-gather.20.cloned.1.call-start = ((), (), s32[]{:S(2)}) async-start(), calls=%async_computation.8 | async-start | bytes 1486848 | tf_op jit(solution)/shard_map/all_gather | solution.py:138
  604.7 48.2 %copy-start.10 = (bf16[88,512]{1,0:T(8,128)(2,1)S(1)}, bf16[88,512]{1,0:T(8,128)(2,1)}, u32[]{:S(2)}) copy-start(bf16[88,512]{1,0:T(8,128)(2,1)} %copy-done.9) | copy-start | bytes 270340
  610.7 100.6 %all-gather.22.cloned.1.call-start = ((), (), s32[]{:S(2)}) async-start(), calls=%async_computation.9 | async-start | bytes 2973696 | tf_op jit(solution)/shard_map/all_gather | solution.py:88
  658.1 4.9 collective-permute-start.2
  663.7 126.4 %all-gather.24.cloned.1.call-start = ((), (), s32[]{:S(2)}) async-start(), calls=%async_computation.10 | async-start | bytes 1486848 | tf_op jit(solution)/shard_map/all_gather | solution.py:138
  741.9 48.2 %copy-start.12 = (bf16[88,512]{1,0:T(8,128)(2,1)S(1)}, bf16[88,512]{1,0:T(8,128)(2,1)}, u32[]{:S(2)}) copy-start(bf16[88,512]{1,0:T(8,128)(2,1)} %copy-done.11) | copy-start | bytes 270340
  748.0 100.6 %all-gather.26.cloned.1.call-start = ((), (), s32[]{:S(2)}) async-start(), calls=%async_computation.11 | async-start | bytes 2973696 | tf_op jit(solution)/shard_map/all_gather | solution.py:88
  795.4 4.9 collective-permute-start.3
  801.0 126.7 %all-gather.28.cloned.1.call-start = ((), (), s32[]{:S(2)}) async-start(), calls=%async_computation.12 | async-start | bytes 1486848 | tf_op jit(solution)/shard_map/all_gather | solution.py:138
  879.5 48.2 %copy-start.8 = (bf16[88,512]{1,0:T(8,128)(2,1)S(1)}, bf16[88,512]{1,0:T(8,128)(2,1)}, u32[]{:S(2)}) copy-start(bf16[88,512]{1,0:T(8,128)(2,1)} %copy-done.7) | copy-start | bytes 270340
  (9 other events, 37.3 us)
Sparse Core Ops, SparseCore 0:
  75.0 103.3 all-gather.29
  334.7 43.3 all-gather.11
  389.1 47.4 all-gather.13
  473.6 41.9 all-gather.15
  526.6 47.4 all-gather.17
  610.9 41.9 all-gather.19
  663.8 47.4 all-gather.21
  748.1 41.9 all-gather.23
  801.1 47.4 all-gather.25
  885.7 41.9 all-gather.27
where the time goes:
time: 948 us; the launch traced here: 941 us
  waiting for transfers between devices  492 us (52%)
  blocking collectives  233 us (25%)
  matrix products  72.1 us (8%)
  local copies, waits for them, and re-layouts  64.4 us (7%)
  starting transfers between devices  49.5 us (5%)
  other arithmetic  15.2 us (2%)
  between operations  14.6 us (2%)
    all_gather x5, waiting for transfers between devices, body(): lax.all_gather(head_mixed, 'tp', axis=1, tiled=True)  212 us
    all_gather x5, waiting for transfers between devices, body(): whole = lax.all_gather(source, 'tp', axis=1, tiled=True)  190 us
    all_gather x5, blocking collectives, body(): kv_whole = lax.all_gather(kv_piece, 'tp', axis=1, tiled=True)  119 us
    all_gather x1, blocking collectives, body(): gain_whole = lax.all_gather(norm_gain, 'tp', axis=1, tiled=True)  114 us
    all_to_all x1, waiting for transfers between devices, body(): lax.all_to_all(query_parts.reshape(flat_count, query_parts.shape[2], quer...  73.6 us
    transpose x3, local copies, waits for them, and re-layouts, split_columns(): weights.reshape(count, height, parts, width // parts).transpose(0, 2, 1, 3)  31.8 us
    unnamed x44, local copies, waits for them, and re-layouts  27.4 us
    dot_general x5, matrix products, body(): jnp.dot(lax.all_gather(head_mixed, 'tp', axis=1, tiled=True), local_outpu...  26.5 us
  transfers between devices with their start and end apart: 18, of which 15 were waited for; matrix products, arithmetic and copies ran while one was open for 7% of the time, Pallas kernels for 0%

commit v1 on v0

v1 whole, which is shorter than its diff:
```python
import functools
import math

import jax
import jax.numpy as jnp
from jax import lax
from jax.experimental import pallas as pl
from jax.experimental.pallas import tpu as pltpu
from jax.sharding import Mesh, PartitionSpec as P


CHIPS = ("z", "x", "y")
PLANE = ("x", "y")
ALL = ("z", "x", "y", "c")
N = 64
HEAD = 128
SEQ = 88
COLS = 256
WIDTH = 16384
ROWS = 112
STEPS = 8
VMEM_LIMIT = 48 * 1024 * 1024
f32 = jnp.float32
bf16 = jnp.bfloat16


def dot(a, b, contract=((1,), (0,))):
    return lax.dot_general(a, b, (contract, ((), ())), preferred_element_type=f32)


def eye_mask():
    rows = lax.broadcasted_iota(jnp.int32, (SEQ, 128), 0)
    lanes = lax.broadcasted_iota(jnp.int32, (SEQ, 128), 1)
    return rows == lanes, lanes <= rows


def prepare(core_ref, x, gain_ref, xg_ref, xgp_ref, ss_ref):
    wide = x.astype(f32)
    eye, _ = eye_mask()
    column = jnp.sum(wide * wide, axis=1, keepdims=True)
    row = jnp.sum(jnp.where(eye, column, 0.0), axis=0, keepdims=True)
    high = row.astype(bf16).astype(f32)
    low = row - high
    which = lax.broadcasted_iota(jnp.int32, (8, 128), 0)
    ss_ref[...] = jnp.where(which == 0, high, jnp.where(which == 1, low, 0.0))
    scaled = wide * gain_ref[...].astype(f32)
    turned = jnp.concatenate([scaled[:, 128:], scaled[:, :128]], axis=1)
    scaled = jnp.where(core_ref[0] == 1, turned, scaled)
    xg_ref[...] = scaled.astype(bf16)
    xgp_ref[...] = jnp.concatenate([scaled, jnp.zeros((128 - SEQ, COLS), f32)], axis=0).astype(bf16)


def project_kernel(lead, core_ref, *refs):
    if lead:
        recv_ref, *refs = refs
    x_ref, gain_ref, wq0, wq1, wk0, wk1, wv0, wv1, *refs = refs
    if lead:
        out_ref, new_ref, acc, xg_ref, xgp_ref, ss_ref, kv_ref = refs
    else:
        out_ref, xg_ref, xgp_ref, ss_ref, kv_ref = refs
    step = pl.program_id(0)
    if lead:

        @pl.when(step == 0)
        def _():
            acc[...] = x_ref[...].astype(f32)

        @pl.when(step < lead)
        def _():
            acc[...] += jnp.sum(recv_ref[...].astype(f32), axis=0)

        @pl.when(step == lead - 1)
        def _():
            new = acc[...].astype(bf16)
            new_ref[...] = new
            prepare(core_ref, new, gain_ref, xg_ref, xgp_ref, ss_ref)
    else:

        @pl.when(step == 0)
        def _():
            prepare(core_ref, x_ref[...], gain_ref, xg_ref, xgp_ref, ss_ref)

    @pl.when(step >= lead)
    def _():
        turn = lax.rem(step - lead, 2)

        @pl.when(turn == 0)
        def _():
            kv_ref[...] = dot(xgp_ref[...], jnp.concatenate([wk0[0], wk1[0]], axis=0)).T

        @pl.when(turn == 1)
        def _():
            kv_ref[...] = dot(xgp_ref[...], jnp.concatenate([wv0[0], wv1[0]], axis=0)).T

        q = dot(xg_ref[...], jnp.concatenate([wq0[0], wq1[0]], axis=0))
        for h in range(8):
            out_ref[h] = jnp.concatenate(
                [kv_ref[16 * h : 16 * h + 16], ss_ref[...], q[:, HEAD * h : HEAD * h + HEAD]], axis=0
            ).astype(bf16)


def project(layer, core, received, x, gain, weights):
    lead = 0 if received is None else STEPS
    at = lambda s: jnp.maximum(s - lead, 0)
    whole = lambda *shape: pl.BlockSpec(shape, lambda s: (0,) * len(shape))
    specs = [pl.BlockSpec(memory_space=pltpu.SMEM)]
    args = [core]
    if lead:
        specs.append(pl.BlockSpec((N // STEPS, SEQ, COLS), lambda s: (jnp.minimum(s, lead - 1), 0, 0)))
        args.append(received)
    specs += [whole(SEQ, COLS), whole(1, COLS)]
    args += [x, gain]
    own, other = weights
    for name, width in (("q", 1024), ("k", 128), ("v", 128)):
        for array in (own[name], other[name]):
            index = layer if array.shape[0] > 1 else 0
            if name == "q":
                index_map = lambda s, index=index: (index, 0, at(s))
            else:
                index_map = lambda s, index=index: (index, 0, at(s) // 2)
            specs.append(pl.BlockSpec((1, 128, width), index_map))
            args.append(array)
    outs = [jax.ShapeDtypeStruct((N, ROWS, 128), bf16)]
    out_specs = [pl.BlockSpec((8, ROWS, 128), lambda s: (at(s), 0, 0))]
    scratch = [
        pltpu.VMEM((SEQ, COLS), bf16),
        pltpu.VMEM((128, COLS), bf16),
        pltpu.VMEM((8, 128), f32),
        pltpu.VMEM((128, 128), f32),
    ]
    if lead:
        outs.append(jax.ShapeDtypeStruct((SEQ, COLS), bf16))
        out_specs.append(whole(SEQ, COLS))
        scratch = [pltpu.VMEM((SEQ, COLS), f32)] + scratch
    result = pl.pallas_call(
        functools.partial(project_kernel, lead),
        grid=(lead + STEPS,),
        in_specs=specs,
        out_specs=out_specs,
        out_shape=outs,
        scratch_shapes=scratch,
        compiler_params=pltpu.CompilerParams(vmem_limit_bytes=VMEM_LIMIT),
        cost_estimate=pl.CostEstimate(
            flops=2 * SEQ * COLS * 9216, bytes_accessed=10_000_000, transcendentals=0
        ),
        name="project",
    )(*args)
    return result if lead else (result[0], x)


def gather_kernel(recv_ref, q_ref, kv_ref, acc):
    step = pl.program_id(0)

    @pl.when(step == 0)
    def _():
        acc[...] = jnp.zeros_like(acc)

    acc[...] += jnp.sum(recv_ref[...].astype(f32), axis=0)

    @pl.when(step == STEPS - 1)
    def _():
        total = acc[16:17] + acc[17:18]
        row = lax.rsqrt(total * (1.0 / WIDTH) + 1e-05)
        eye, _ = eye_mask()
        column = jnp.sum(jnp.where(eye, row, 0.0), axis=1, keepdims=True)
        q_ref[...] = (acc[24:] * column).astype(bf16)
        kv_ref[...] = jnp.broadcast_to((acc[:16] * row)[None], kv_ref.shape).astype(bf16)


def gather(received):
    return pl.pallas_call(
        gather_kernel,
        grid=(STEPS,),
        in_specs=[pl.BlockSpec((N // STEPS, ROWS, 128), lambda s: (s, 0, 0))],
        out_specs=[
            pl.BlockSpec((SEQ, HEAD), lambda s: (0, 0)),
            pl.BlockSpec((16, 16, 128), lambda s: (0, 0, 0)),
        ],
        out_shape=[
            jax.ShapeDtypeStruct((SEQ, HEAD), bf16),
            jax.ShapeDtypeStruct((16, 16, 128), bf16),
        ],
        scratch_shapes=[pltpu.VMEM((ROWS, 128), f32)],
        compiler_params=pltpu.CompilerParams(vmem_limit_bytes=VMEM_LIMIT),
        cost_estimate=pl.CostEstimate(flops=2_000_000, bytes_accessed=2_000_000, transcendentals=0),
        name="collect",
    )(received)


def attend_kernel(core_ref, q_ref, kv_ref, wo0, wo1, out_ref, mixed_ref):
    step = pl.program_id(0)

    @pl.when(step == 0)
    def _():
        kv = kv_ref[...].reshape(256, 128)
        _, causal = eye_mask()
        scores = dot(q_ref[...], kv[:128]) * (1.0 / math.sqrt(HEAD))
        weights = jnp.where(causal, jnp.exp(scores), 0.0)
        shares = (weights / jnp.sum(weights, axis=1, keepdims=True)).astype(bf16)
        mixed = dot(shares, kv[128:], ((1,), (1,)))
        turned = jnp.concatenate([mixed[:, 64:], mixed[:, :64]], axis=1)
        mixed_ref[...] = jnp.where(core_ref[0] == 1, turned, mixed).astype(bf16)

    o = dot(mixed_ref[...], jnp.concatenate([wo0[0], wo1[0]], axis=0))
    for i in range(8):
        out_ref[i] = o[:, COLS * i : COLS * i + COLS].astype(bf16)


def attend(layer, core, q, kv, weights):
    arrays = [w["o"] for w in weights]
    return pl.pallas_call(
        attend_kernel,
        grid=(STEPS,),
        in_specs=[
            pl.BlockSpec(memory_space=pltpu.SMEM),
            pl.BlockSpec((SEQ, HEAD), lambda s: (0, 0)),
            pl.BlockSpec((16, 16, 128), lambda s: (0, 0, 0)),
        ]
        + [
            pl.BlockSpec((1, 64, 2048), lambda s, index=layer if w.shape[0] > 1 else 0: (index, 0, s))
            for w in arrays
        ],
        out_specs=pl.BlockSpec((8, SEQ, COLS), lambda s: (s, 0, 0)),
        out_shape=jax.ShapeDtypeStruct((N, SEQ, COLS), bf16),
        scratch_shapes=[pltpu.VMEM((SEQ, HEAD), bf16)],
        compiler_params=pltpu.CompilerParams(vmem_limit_bytes=VMEM_LIMIT),
        cost_estimate=pl.CostEstimate(
            flops=2 * SEQ * HEAD * WIDTH, bytes_accessed=7_000_000, transcendentals=0
        ),
        name="attend",
    )(core, q, kv, *arrays)


def close_kernel(recv_ref, x_ref, out_ref, acc):
    step = pl.program_id(0)

    @pl.when(step == 0)
    def _():
        acc[...] = x_ref[...].astype(f32)

    acc[...] += jnp.sum(recv_ref[...].astype(f32), axis=0)

    @pl.when(step == STEPS - 1)
    def _():
        out_ref[...] = acc[...].astype(bf16)


def close(received, x):
    return pl.pallas_call(
        close_kernel,
        grid=(STEPS,),
        in_specs=[
            pl.BlockSpec((N // STEPS, SEQ, COLS), lambda s: (s, 0, 0)),
            pl.BlockSpec((SEQ, COLS), lambda s: (0, 0)),
        ],
        out_specs=pl.BlockSpec((SEQ, COLS), lambda s: (0, 0)),
        out_shape=jax.ShapeDtypeStruct((SEQ, COLS), bf16),
        scratch_shapes=[pltpu.VMEM((SEQ, COLS), f32)],
        compiler_params=pltpu.CompilerParams(vmem_limit_bytes=VMEM_LIMIT),
        cost_estimate=pl.CostEstimate(flops=3_000_000, bytes_accessed=3_000_000, transcendentals=0),
        name="close",
    )(received, x)


def exchange(value, axes):
    return lax.all_to_all(value, axes, 0, 0, tiled=True)


def swap(value):
    return lax.ppermute(value, "c", [(0, 1), (1, 0)])


def body(entering, norm_gain, query_weight, key_matrix, value_matrix, output_weight):
    plane = lax.axis_index("z")
    core = lax.axis_index("c")
    half = lax.rem(lax.axis_index("y"), 2)
    slot = 2 * core + half
    core_array = core.astype(jnp.int32).reshape(1)

    x = None
    for m in range(2):
        for h in range(2):
            pairs = [(32 * (i // 16) + i // 2, 2 * i + m) for i in range(h, N, 2)]
            piece = lax.ppermute(entering[m, :, COLS * h : COLS * h + COLS], ALL, pairs)
            x = piece if x is None else x + piece
    rounds = []
    for k in range(4):
        pairs = [
            (32 * ((2 * c + i % 2 + k) % 4) + i // 2, 2 * i + c) for i in range(N) for c in range(2)
        ]
        piece = lax.dynamic_slice_in_dim(norm_gain, lax.rem(plane + 4 - k, 2) * COLS, COLS, 1)
        rounds.append(lax.ppermute(piece, ALL, pairs))
    rounds = jnp.stack(rounds)
    gains = [
        lax.dynamic_index_in_dim(rounds, lax.rem(layer - slot + 4, 4), 0, keepdims=False)
        for layer in range(4)
    ]

    own = dict(q=query_weight, k=key_matrix, v=value_matrix, o=output_weight)
    other_k = swap(key_matrix)
    other_v = swap(value_matrix)
    others = [
        dict(
            q=swap(query_weight[layer : layer + 1]),
            k=other_k,
            v=other_v,
            o=swap(output_weight[layer : layer + 1]),
        )
        for layer in range(4)
    ]

    received = None
    states = []
    for layer in range(4):
        weights = (own, others[layer])
        partial, x = project(layer, core_array, received, x, gains[layer], weights)
        if layer:
            states.append(x)
        q, kv = gather(exchange(partial, CHIPS))
        received = exchange(attend(layer, core_array, q, exchange(kv, PLANE), weights), CHIPS)
    states.append(close(received, x))

    states = jnp.stack(states)
    rounds = []
    for k in range(4):
        pairs = [
            (2 * i + c, 32 * ((2 * c + i % 2 + k) % 4) + i // 2) for i in range(N) for c in range(2)
        ]
        piece = lax.dynamic_index_in_dim(states, lax.rem(slot + k, 4), 0, keepdims=False)
        rounds.append(lax.ppermute(piece, ALL, pairs))
    rounds = jnp.stack(rounds)
    pieces = [
        lax.dynamic_index_in_dim(rounds, lax.rem(plane - s + 4, 4), 0, keepdims=False) for s in range(4)
    ]
    return jnp.stack(
        [jnp.concatenate(pieces[:2], axis=1), jnp.concatenate(pieces[2:], axis=1)]
    )[None]


def solution(mesh):
    fine = Mesh(mesh.devices.reshape(4, 4, 4, 2), ALL)
    tp = ("x", "y", "c")
    rows = P(None, ALL, None)
    return jax.shard_map(
        body,
        mesh=fine,
        in_specs=(P(None, None, tp), P("z", tp), rows, rows, rows, rows),
        out_specs=P("z", None, None, tp),
        check_vma=False,
    )
```

time: 948 us -> 479 us (0.51)
  waiting for transfers between devices: 492 us -> 149 us
  blocking collectives: 233 us -> 119 us
  matrix products: 72.1 us -> 0 us
  Pallas kernels: 0 us -> 71.6 us
  starting transfers between devices: 49.5 us -> 111 us
  local copies, waits for them, and re-layouts: 64.4 us -> 23.2 us
  other arithmetic: 15.2 us -> 0.78 us
  between operations: 14.6 us -> 0.38 us
    all_gather x10 -> x0, waiting for transfers between devices: 402 us -> none  [the longest x5 212 us: body(): lax.all_gather(head_mixed, 'tp', axis=1, tiled=True)]
    all_gather x6 -> x0, blocking collectives: 233 us -> none  [the longest x5 119 us: body(): kv_whole = lax.all_gather(kv_piece, 'tp', axis=1, tiled=True)]
    all_to_all x0 -> x4, blocking collectives: none -> 119 us  [exchange(): return lax.all_to_all(value, axes, 0, 0, tiled=True)]
    dot_general x30 -> x0, matrix products: 72.1 us -> none  [the longest x5 26.5 us: body(): jnp.dot(lax.all_gather(head_mixed, 'tp', axis=1, tiled=True), local_outpu...]
    pallas_call x0 -> x13, Pallas kernels: none -> 71.6 us  [the longest x4 38.3 us: project(): pl.pallas_call(functools.partial(project_kernel, lead), grid=(lead + STEP...]
    ppermute x4 -> x22, starting transfers between devices: 12.7 us -> 59.5 us  [the longest x8 33.6 us: body(): rounds.append(lax.ppermute(piece, ALL, pairs))]
    all_to_all x4 -> x8, waiting for transfers between devices: 83.2 us -> 119 us  [exchange(): return lax.all_to_all(value, axes, 0, 0, tiled=True)]
    transpose x5 -> x0, local copies, waits for them, and re-layouts: 33.8 us -> none  [the longest x3 31.8 us: split_columns(): weights.reshape(count, height, parts, width // parts).transpose(0, 2, 1, 3)]
  transfers between devices with their start and end apart: 18 -> 30, of which waited for: 15 -> 16; matrix products, arithmetic and copies ran while one was open for 7% -> 2% of each run, Pallas kernels for 0% -> 9%
where the time goes in v1:
time: 479 us; the launch traced here: 474 us
  waiting for transfers between devices  149 us (31%)
  blocking collectives  119 us (25%)
  starting transfers between devices  111 us (23%)
  Pallas kernels  71.6 us (15%)
  local copies, waits for them, and re-layouts  23.2 us (5%)
    all_to_all x8, waiting for transfers between devices, exchange(): return lax.all_to_all(value, axes, 0, 0, tiled=True)  119 us
    all_to_all x4, blocking collectives, exchange(): return lax.all_to_all(value, axes, 0, 0, tiled=True)  119 us
    all_to_all x8, starting transfers between devices, exchange(): return lax.all_to_all(value, axes, 0, 0, tiled=True)  51.4 us
    pallas_call x4, Pallas kernels, project(): pl.pallas_call(functools.partial(project_kernel, lead), grid=(lead + STEP...  38.3 us
    ppermute x8, starting transfers between devices, body(): rounds.append(lax.ppermute(piece, ALL, pairs))  33.6 us
    pallas_call x4, Pallas kernels, attend(): pl.pallas_call(attend_kernel, grid=(STEPS,), in_specs=[pl.BlockSpec(memor...  28.3 us
    ppermute x10, starting transfers between devices, swap(): return lax.ppermute(value, 'c', [(0, 1), (1, 0)])  22.6 us
    ppermute x10, waiting for transfers between devices, swap(): return lax.ppermute(value, 'c', [(0, 1), (1, 0)])  17.9 us
  transfers between devices with their start and end apart: 30, of which 16 were waited for; matrix products, arithmetic and copies ran while one was open for 2% of the time, Pallas kernels for 9%

profile of v1, /device:TPU:5, one launch (start us, length us, event | category | flops | bytes accessed | tf_op | source)
XLA Modules:
  0.0 474.1 jit_solution(11763186396167355542)
XLA Ops:
  0.8 8.6 %collective-permute-start.4 = (bf16[1,256]{1,0:T(2,128)(2,1)S(1)}, bf16[1,256]{1,0:T(2,128)(2,1)S(1)}, u32[]{:S(2)}, u32[]{:S(2)}) collective-permute-start(bf16[1,256]{1,0:T(2,128)(2,1)S(1)} %get-tuple-element.57), channel_id=1, source_target_pairs={{0,0},{64,1},{32,2},{96,3},{1,4},{65,5},{33,6},{97,7},{2,8},{66,9}... | collective-permute-start | bytes 1544 | tf_op jit(solution)/shard_map/ppermute | solution.py:292
  11.0 6.5 %fusion.5 = (bf16[1,128,8192]{2,1,0:T(8,128)(2,1)}, bf16[1,128,8192]{2,1,0:T(8,128)(2,1)}, bf16[1,128,8192]{2,1,0:T(8,128)(2,1)}, bf16[1,128,8192]{2,1,0:T(8,128)(2,1)}) fusion(bf16[4,128,8192]{2,1,0:T(8,128)(2,1)} %refs_3_.5), kind=kLoop, calls=%fused_computation.32 | loop fusion | bytes 16777216 | tf_op jit(solution)/shard_map/slice | solution.py:304
  23.1 6.2 %collective-permute-start.7 = (bf16[1,256]{1,0:T(2,128)(2,1)S(1)}, bf16[1,256]{1,0:T(2,128)(2,1)S(1)}, u32[]{:S(2)}, u32[]{:S(2)}) collective-permute-start(bf16[1,256]{1,0:T(2,128)(2,1)S(1)} %get-tuple-element.59), channel_id=1, source_target_pairs={{96,0},{32,1},{0,2},{64,3},{97,4},{33,5},{1,6},{65,7},{98,8},{34,9... | collective-permute-start | bytes 1544 | tf_op jit(solution)/shard_map/ppermute | solution.py:292
  38.9 8.1 %collective-permute-start.11 = (bf16[1,64,16384]{2,1,0:T(8,128)(2,1)}, bf16[1,64,16384]{2,1,0:T(8,128)(2,1)}, u32[]{:S(2)}, u32[]{:S(2)}) collective-permute-start(bf16[1,64,16384]{2,1,0:T(8,128)(2,1)} %get-tuple-element.36), channel_id=1, source_target_pairs={{0,1},{1,0},{2,3},{3,2},{4,5},{5,4},{6,7},{7,6},{8,9},{9,8},{10,11... | collective-permute-start | bytes 6291464 | tf_op jit(solution)/shard_map/ppermute | solution.py:270
  48.4 6.8 %project.4 = bf16[64,112,128]{2,1,0:T(8,128)(2,1)S(1)} custom-call(s32[1]{0:T(128)} %bitcast.core_ref, bf16[88,256]{1,0:T(8,128)(2,1)S(1)} %add_add_fusion.refs_0_.refs_1_, bf16[1,256]{1,0:T(2,128)(2,1)S(1)} %get-tuple-element.56.refs_1_, bf16[4,128,8192]{2,1,0:T(8,128)(2,1)} %refs_3_.5, bf16[1,128,8192]{2,1,0:T(8,128)(2,1)} %collective-permute-done.8.refs_3_, ...), custom_call_target="tpu_custom_call" | custom-call | flops 415236096 | bytes 10000000 | tf_op jit(solution)/shard_map/project/pallas_call | solution.py:135
  55.2 31.2 %all_to_all.60.recv_ref = bf16[64,112,128]{2,1,0:T(8,128)(2,1)S(1)} all-to-all(bf16[64,112,128]{2,1,0:T(8,128)(2,1)S(1)} %project.4), channel_id=1, replica_groups=mesh['z'=4,'x'=4,'y'=4,'c'=2] {'z','x','y'}, dimensions={0} | all-to-all | bytes 3670016 | tf_op jit(solution)/shard_map/all_to_all | solution.py:266
  97.7 7.4 %attend.4 = bf16[64,88,256]{2,1,0:T(8,128)(2,1)} custom-call(s32[1]{0:T(128)} %bitcast.core_ref, bf16[88,128]{1,0:T(8,128)(2,1)S(1)} %get-tuple-element.19.q_ref, bf16[16,16,128]{2,1,0:T(8,128)(2,1)S(1)} %all-to-all-done.1.kv_ref, bf16[4,64,16384]{2,1,0:T(8,128)(2,1)} %wo0.7, bf16[1,64,16384]{2,1,0:T(8,128)(2,1)} %collective-permute-done.11.wo1), custom_call_target="tpu_custom_call" | custom-call | flops 369098752 | bytes 7000000 | tf_op jit(solution)/shard_map/attend/pallas_call | solution.py:211
  105.2 7.0 %all-to-all-start.2 = ((bf16[64,88,256]{2,1,0:T(8,128)(2,1)}), bf16[64,88,256]{2,1,0:T(8,128)(2,1)}, u32[]{:S(2)}, u32[]{:S(2)}) async-start(bf16[64,88,256]{2,1,0:T(8,128)(2,1)} %attend.4), calls=%async_computation.2 | async-start | bytes 5767168 | tf_op jit(solution)/shard_map/all_to_all | solution.py:266
  122.6 25.8 %all-to-all-done.2.refs_0_ = bf16[64,88,256]{2,1,0:T(8,128)(2,1)} async-done(((bf16[64,88,256]{2,1,0:T(8,128)(2,1)}), bf16[64,88,256]{2,1,0:T(8,128)(2,1)}, u32[]{:S(2)}, u32[]{:S(2)}) %all-to-all-start.2) | async-done | bytes 2883616 | tf_op jit(solution)/shard_map/all_to_all | solution.py:266
  150.0 10.5 %project.5 = (bf16[64,112,128]{2,1,0:T(8,128)(2,1)S(1)}, bf16[88,256]{1,0:T(8,128)(2,1)S(1)}) custom-call(s32[1]{0:T(128)} %bitcast.core_ref, bf16[64,88,256]{2,1,0:T(8,128)(2,1)} %all-to-all-done.2.refs_0_, bf16[88,256]{1,0:T(8,128)(2,1)S(1)} %add_add_fusion.refs_0_.refs_1_, bf16[1,256]{1,0:T(2,128)(2,1)S(1)} %get-tuple-element.55.refs_2_, ...), custom_call_target="tpu_custom_call" | custom-call | flops 415236096 | bytes 10000000 | tf_op jit(solution)/shard_map/project/pallas_call | solution.py:135
  160.5 27.1 %all_to_all.61.recv_ref = bf16[64,112,128]{2,1,0:T(8,128)(2,1)S(1)} all-to-all(bf16[64,112,128]{2,1,0:T(8,128)(2,1)S(1)} %get-tuple-element.22), channel_id=1, replica_groups=mesh['z'=4,'x'=4,'y'=4,'c'=2] {'z','x','y'}, dimensions={0} | all-to-all | bytes 3670016 | tf_op jit(solution)/shard_map/all_to_all | solution.py:266
  199.4 7.4 %attend.5 = bf16[64,88,256]{2,1,0:T(8,128)(2,1)} custom-call(s32[1]{0:T(128)} %bitcast.core_ref, bf16[88,128]{1,0:T(8,128)(2,1)S(1)} %get-tuple-element.23.q_ref, bf16[16,16,128]{2,1,0:T(8,128)(2,1)S(1)} %all-to-all-done.4.kv_ref, bf16[4,64,16384]{2,1,0:T(8,128)(2,1)} %wo0.7, bf16[1,64,16384]{2,1,0:T(8,128)(2,1)} %collective-permute-done.13.wo1), custom_call_target="tpu_custom_call" | custom-call | flops 369098752 | bytes 7000000 | tf_op jit(solution)/shard_map/attend/pallas_call | solution.py:211
  206.8 7.0 %all-to-all-start.5 = ((bf16[64,88,256]{2,1,0:T(8,128)(2,1)}), bf16[64,88,256]{2,1,0:T(8,128)(2,1)}, u32[]{:S(2)}, u32[]{:S(2)}) async-start(bf16[64,88,256]{2,1,0:T(8,128)(2,1)} %attend.5), calls=%async_computation.5 | async-start | bytes 5767168 | tf_op jit(solution)/shard_map/all_to_all | solution.py:266
  226.5 20.7 %all-to-all-done.5.refs_0_ = bf16[64,88,256]{2,1,0:T(8,128)(2,1)} async-done(((bf16[64,88,256]{2,1,0:T(8,128)(2,1)}), bf16[64,88,256]{2,1,0:T(8,128)(2,1)}, u32[]{:S(2)}, u32[]{:S(2)}) %all-to-all-start.5) | async-done | bytes 2883616 | tf_op jit(solution)/shard_map/all_to_all | solution.py:266
  248.8 10.5 %project.6 = (bf16[64,112,128]{2,1,0:T(8,128)(2,1)S(1)}, bf16[88,256]{1,0:T(8,128)(2,1)S(1)}) custom-call(s32[1]{0:T(128)} %bitcast.core_ref, bf16[64,88,256]{2,1,0:T(8,128)(2,1)} %all-to-all-done.5.refs_0_, bf16[88,256]{1,0:T(8,128)(2,1)S(1)} %get-tuple-element.21.refs_1_, bf16[1,256]{1,0:T(2,128)(2,1)S(1)} %get-tuple-element.54.refs_2_, ...), custom_call_target="tpu_custom_call" | custom-call | flops 415236096 | bytes 10000000 | tf_op jit(solution)/shard_map/project/pallas_call | solution.py:135
  259.3 30.5 %all_to_all.62.recv_ref = bf16[64,112,128]{2,1,0:T(8,128)(2,1)S(1)} all-to-all(bf16[64,112,128]{2,1,0:T(8,128)(2,1)S(1)} %get-tuple-element.26), channel_id=1, replica_groups=mesh['z'=4,'x'=4,'y'=4,'c'=2] {'z','x','y'}, dimensions={0} | all-to-all | bytes 3670016 | tf_op jit(solution)/shard_map/all_to_all | solution.py:266
  301.7 7.4 %attend.6 = bf16[64,88,256]{2,1,0:T(8,128)(2,1)} custom-call(s32[1]{0:T(128)} %bitcast.core_ref, bf16[88,128]{1,0:T(8,128)(2,1)S(1)} %get-tuple-element.27.q_ref, bf16[16,16,128]{2,1,0:T(8,128)(2,1)S(1)} %all-to-all-done.7.kv_ref, bf16[4,64,16384]{2,1,0:T(8,128)(2,1)} %wo0.7, bf16[1,64,16384]{2,1,0:T(8,128)(2,1)} %collective-permute-done.15.wo1), custom_call_target="tpu_custom_call" | custom-call | flops 369098752 | bytes 7000000 | tf_op jit(solution)/shard_map/attend/pallas_call | solution.py:211
  309.1 7.0 %all-to-all-start.8 = ((bf16[64,88,256]{2,1,0:T(8,128)(2,1)}), bf16[64,88,256]{2,1,0:T(8,128)(2,1)}, u32[]{:S(2)}, u32[]{:S(2)}) async-start(bf16[64,88,256]{2,1,0:T(8,128)(2,1)} %attend.6), calls=%async_computation.8 | async-start | bytes 5767168 | tf_op jit(solution)/shard_map/all_to_all | solution.py:266
  329.0 20.8 %all-to-all-done.8.refs_0_ = bf16[64,88,256]{2,1,0:T(8,128)(2,1)} async-done(((bf16[64,88,256]{2,1,0:T(8,128)(2,1)}), bf16[64,88,256]{2,1,0:T(8,128)(2,1)}, u32[]{:S(2)}, u32[]{:S(2)}) %all-to-all-start.8) | async-done | bytes 2883616 | tf_op jit(solution)/shard_map/all_to_all | solution.py:266
  351.3 10.5 %project.7 = (bf16[64,112,128]{2,1,0:T(8,128)(2,1)S(1)}, bf16[88,256]{1,0:T(8,128)(2,1)S(1)}) custom-call(s32[1]{0:T(128)} %bitcast.core_ref, bf16[64,88,256]{2,1,0:T(8,128)(2,1)} %all-to-all-done.8.refs_0_, bf16[88,256]{1,0:T(8,128)(2,1)S(1)} %get-tuple-element.25.refs_1_, bf16[1,256]{1,0:T(2,128)(2,1)S(1)} %get-tuple-element.53.refs_2_, ...), custom_call_target="tpu_custom_call" | custom-call | flops 415236096 | bytes 10000000 | tf_op jit(solution)/shard_map/project/pallas_call | solution.py:135
  361.8 29.8 %all_to_all.63.recv_ref = bf16[64,112,128]{2,1,0:T(8,128)(2,1)S(1)} all-to-all(bf16[64,112,128]{2,1,0:T(8,128)(2,1)S(1)} %get-tuple-element.30), channel_id=1, replica_groups=mesh['z'=4,'x'=4,'y'=4,'c'=2] {'z','x','y'}, dimensions={0} | all-to-all | bytes 3670016 | tf_op jit(solution)/shard_map/all_to_all | solution.py:266
  411.0 6.2 %all-to-all-start.11 = ((bf16[64,88,256]{2,1,0:T(8,128)(2,1)}), bf16[64,88,256]{2,1,0:T(8,128)(2,1)S(1)}, u32[]{:S(2)}, u32[]{:S(2)}) async-start(bf16[64,88,256]{2,1,0:T(8,128)(2,1)} %copy-done), calls=%async_computation.11 | async-start | bytes 5767168 | tf_op jit(solution)/shard_map/all_to_all | solution.py:266
  417.3 33.3 %all-to-all-done.11.recv_ref = bf16[64,88,256]{2,1,0:T(8,128)(2,1)S(1)} async-done(((bf16[64,88,256]{2,1,0:T(8,128)(2,1)}), bf16[64,88,256]{2,1,0:T(8,128)(2,1)S(1)}, u32[]{:S(2)}, u32[]{:S(2)}) %all-to-all-start.11) | async-done | bytes 2883616 | tf_op jit(solution)/shard_map/all_to_all | solution.py:266
  451.2 9.0 %collective-permute-start.18 = (bf16[88,256]{1,0:T(8,128)(2,1)S(1)}, bf16[88,256]{1,0:T(8,128)(2,1)S(1)}, u32[]{:S(2)}, u32[]{:S(2)}) collective-permute-start(bf16[88,256]{1,0:T(8,128)(2,1)S(1)} %get-tuple-element.45), channel_id=1, source_target_pairs={{0,0},{1,64},{2,32},{3,96},{4,1},{5,65},{6,33},{7,97},{8,2},{9,66}... | collective-permute-start | bytes 135176 | tf_op jit(solution)/shard_map/ppermute | solution.py:330
  (88 shorter events, 128.3 us)
Async XLA Ops:
  0.8 22.3 %collective-permute-start.4 = (bf16[1,256]{1,0:T(2,128)(2,1)S(1)}, bf16[1,256]{1,0:T(2,128)(2,1)S(1)}, u32[]{:S(2)}, u32[]{:S(2)}) collective-permute-start(bf16[1,256]{1,0:T(2,128)(2,1)S(1)} %get-tuple-element.57), channel_id=1, source_target_pairs={{0,0},{64,1},{32,2},{96,3},{1,4},{65,5},{33,6},{97,7},{2,8},{66,9}... | collective-permute-start | bytes 1544 | tf_op jit(solution)/shard_map/ppermute | solution.py:292
  9.4 19.9 %collective-permute-start.5 = (bf16[1,256]{1,0:T(2,128)(2,1)S(1)}, bf16[1,256]{1,0:T(2,128)(2,1)S(1)}, u32[]{:S(2)}, u32[]{:S(2)}) collective-permute-start(bf16[1,256]{1,0:T(2,128)(2,1)S(1)} %get-tuple-element.58), channel_id=1, source_target_pairs={{32,0},{96,1},{64,2},{0,3},{33,4},{97,5},{65,6},{1,7},{34,8},{98,9... | collective-permute-start | bytes 1544 | tf_op jit(solution)/shard_map/ppermute | solution.py:292
  10.5 37.8 %collective-permute-start.9 = (bf16[4,128,512]{2,1,0:T(8,128)(2,1)}, bf16[4,128,512]{2,1,0:T(8,128)(2,1)S(1)}, u32[]{:S(2)}, u32[]{:S(2)}) collective-permute-start(bf16[4,128,512]{2,1,0:T(8,128)(2,1)} %refs_5_.5), channel_id=1, source_target_pairs={{0,1},{1,0},{2,3},{3,2},{4,5},{5,4},{6,7},{7,6},{8,9},{9,8},{10,11... | collective-permute-start | bytes 1572872 | tf_op jit(solution)/shard_map/ppermute | solution.py:270
  10.5 37.8 %collective-permute-start.10 = (bf16[4,128,512]{2,1,0:T(8,128)(2,1)}, bf16[4,128,512]{2,1,0:T(8,128)(2,1)S(1)}, u32[]{:S(2)}, u32[]{:S(2)}) collective-permute-start(bf16[4,128,512]{2,1,0:T(8,128)(2,1)} %refs_7_.5), channel_id=1, source_target_pairs={{0,1},{1,0},{2,3},{3,2},{4,5},{5,4},{6,7},{7,6},{8,9},{9,8},{10,11... | collective-permute-start | bytes 1572872 | tf_op jit(solution)/shard_map/ppermute | solution.py:270
  17.5 30.8 %collective-permute-start.8 = (bf16[1,128,8192]{2,1,0:T(8,128)(2,1)}, bf16[1,128,8192]{2,1,0:T(8,128)(2,1)}, u32[]{:S(2)}, u32[]{:S(2)}) collective-permute-start(bf16[1,128,8192]{2,1,0:T(8,128)(2,1)} %get-tuple-element.40), channel_id=1, source_target_pairs={{0,1},{1,0},{2,3},{3,2},{4,5},{5,4},{6,7},{7,6},{8,9},{9,8},{10,11... | collective-permute-start | bytes 6291464 | tf_op jit(solution)/shard_map/ppermute | solution.py:270
  37.5 10.8 %collective-permute-start.2 = (bf16[88,256]{1,0:T(8,128)(2,1)S(1)}, bf16[88,256]{1,0:T(8,128)(2,1)S(1)}, u32[]{:S(2)}, u32[]{:S(2)}) collective-permute-start(bf16[88,256]{1,0:T(8,128)(2,1)S(1)} %get-tuple-element.52), channel_id=1, source_target_pairs={{0,1},{1,5},{2,9},{3,13},{4,17},{5,21},{6,25},{7,29},{40,33},{41,3... | collective-permute-start | bytes 135176 | tf_op jit(solution)/shard_map/ppermute | solution.py:284
  38.9 54.3 %collective-permute-start.11 = (bf16[1,64,16384]{2,1,0:T(8,128)(2,1)}, bf16[1,64,16384]{2,1,0:T(8,128)(2,1)}, u32[]{:S(2)}, u32[]{:S(2)}) collective-permute-start(bf16[1,64,16384]{2,1,0:T(8,128)(2,1)} %get-tuple-element.36), channel_id=1, source_target_pairs={{0,1},{1,0},{2,3},{3,2},{4,5},{5,4},{6,7},{7,6},{8,9},{9,8},{10,11... | collective-permute-start | bytes 6291464 | tf_op jit(solution)/shard_map/ppermute | solution.py:270
  87.4 10.3 %all-to-all-start.1 = ((bf16[16,16,128]{2,1,0:T(8,128)(2,1)}), bf16[16,16,128]{2,1,0:T(8,128)(2,1)S(1)}, u32[]{:S(2)}, u32[]{:S(2)}) async-start(bf16[16,16,128]{2,1,0:T(8,128)(2,1)} %get-tuple-element.20), calls=%async_computation.1 | async-start | bytes 131072 | tf_op jit(solution)/shard_map/all_to_all | solution.py:266
  105.2 43.3 %all-to-all-start.2 = ((bf16[64,88,256]{2,1,0:T(8,128)(2,1)}), bf16[64,88,256]{2,1,0:T(8,128)(2,1)}, u32[]{:S(2)}, u32[]{:S(2)}) async-start(bf16[64,88,256]{2,1,0:T(8,128)(2,1)} %attend.4), calls=%async_computation.2 | async-start | bytes 5767168 | tf_op jit(solution)/shard_map/all_to_all | solution.py:266
  115.2 79.6 %collective-permute-start.13 = (bf16[1,64,16384]{2,1,0:T(8,128)(2,1)}, bf16[1,64,16384]{2,1,0:T(8,128)(2,1)}, u32[]{:S(2)}, u32[]{:S(2)}) collective-permute-start(bf16[1,64,16384]{2,1,0:T(8,128)(2,1)} %get-tuple-element.35), channel_id=1, source_target_pairs={{0,1},{1,0},{2,3},{3,2},{4,5},{5,4},{6,7},{7,6},{8,9},{9,8},{10,11... | collective-permute-start | bytes 6291464 | tf_op jit(solution)/shard_map/ppermute | solution.py:270
  188.7 10.7 %all-to-all-start.4 = ((bf16[16,16,128]{2,1,0:T(8,128)(2,1)}), bf16[16,16,128]{2,1,0:T(8,128)(2,1)S(1)}, u32[]{:S(2)}, u32[]{:S(2)}) async-start(bf16[16,16,128]{2,1,0:T(8,128)(2,1)} %get-tuple-element.24), calls=%async_computation.4 | async-start | bytes 131072 | tf_op jit(solution)/shard_map/all_to_all | solution.py:266
  206.8 40.4 %all-to-all-start.5 = ((bf16[64,88,256]{2,1,0:T(8,128)(2,1)}), bf16[64,88,256]{2,1,0:T(8,128)(2,1)}, u32[]{:S(2)}, u32[]{:S(2)}) async-start(bf16[64,88,256]{2,1,0:T(8,128)(2,1)} %attend.5), calls=%async_computation.5 | async-start | bytes 5767168 | tf_op jit(solution)/shard_map/all_to_all | solution.py:266
  213.9 11.3 %collective-permute-start.14 = (bf16[1,128,8192]{2,1,0:T(8,128)(2,1)}, bf16[1,128,8192]{2,1,0:T(8,128)(2,1)S(1)}, u32[]{:S(2)}, u32[]{:S(2)}) collective-permute-start(bf16[1,128,8192]{2,1,0:T(8,128)(2,1)} %get-tuple-element.38), channel_id=1, source_target_pairs={{0,1},{1,0},{2,3},{3,2},{4,5},{5,4},{6,7},{7,6},{8,9},{9,8},{10,11... | collective-permute-start | bytes 6291464 | tf_op jit(solution)/shard_map/ppermute | solution.py:270
  219.1 78.0 %collective-permute-start.15 = (bf16[1,64,16384]{2,1,0:T(8,128)(2,1)}, bf16[1,64,16384]{2,1,0:T(8,128)(2,1)}, u32[]{:S(2)}, u32[]{:S(2)}) collective-permute-start(bf16[1,64,16384]{2,1,0:T(8,128)(2,1)} %get-tuple-element.34), channel_id=1, source_target_pairs={{0,1},{1,0},{2,3},{3,2},{4,5},{5,4},{6,7},{7,6},{8,9},{9,8},{10,11... | collective-permute-start | bytes 6291464 | tf_op jit(solution)/shard_map/ppermute | solution.py:270
  291.0 10.7 %all-to-all-start.7 = ((bf16[16,16,128]{2,1,0:T(8,128)(2,1)}), bf16[16,16,128]{2,1,0:T(8,128)(2,1)S(1)}, u32[]{:S(2)}, u32[]{:S(2)}) async-start(bf16[16,16,128]{2,1,0:T(8,128)(2,1)} %get-tuple-element.28), calls=%async_computation.7 | async-start | bytes 131072 | tf_op jit(solution)/shard_map/all_to_all | solution.py:266
  309.1 40.6 %all-to-all-start.8 = ((bf16[64,88,256]{2,1,0:T(8,128)(2,1)}), bf16[64,88,256]{2,1,0:T(8,128)(2,1)}, u32[]{:S(2)}, u32[]{:S(2)}) async-start(bf16[64,88,256]{2,1,0:T(8,128)(2,1)} %attend.6), calls=%async_computation.8 | async-start | bytes 5767168 | tf_op jit(solution)/shard_map/all_to_all | solution.py:266
  316.1 11.5 %collective-permute-start.16 = (bf16[1,128,8192]{2,1,0:T(8,128)(2,1)}, bf16[1,128,8192]{2,1,0:T(8,128)(2,1)S(1)}, u32[]{:S(2)}, u32[]{:S(2)}) collective-permute-start(bf16[1,128,8192]{2,1,0:T(8,128)(2,1)} %get-tuple-element.37), channel_id=1, source_target_pairs={{0,1},{1,0},{2,3},{3,2},{4,5},{5,4},{6,7},{7,6},{8,9},{9,8},{10,11... | collective-permute-start | bytes 6291464 | tf_op jit(solution)/shard_map/ppermute | solution.py:270
  321.5 77.4 %collective-permute-start.17 = (bf16[1,64,16384]{2,1,0:T(8,128)(2,1)}, bf16[1,64,16384]{2,1,0:T(8,128)(2,1)}, u32[]{:S(2)}, u32[]{:S(2)}) collective-permute-start(bf16[1,64,16384]{2,1,0:T(8,128)(2,1)} %get-tuple-element.33), channel_id=1, source_target_pairs={{0,1},{1,0},{2,3},{3,2},{4,5},{5,4},{6,7},{7,6},{8,9},{9,8},{10,11... | collective-permute-start | bytes 6291464 | tf_op jit(solution)/shard_map/ppermute | solution.py:270
  392.8 10.7 %all-to-all-start.10 = ((bf16[16,16,128]{2,1,0:T(8,128)(2,1)}), bf16[16,16,128]{2,1,0:T(8,128)(2,1)S(1)}, u32[]{:S(2)}, u32[]{:S(2)}) async-start(bf16[16,16,128]{2,1,0:T(8,128)(2,1)} %get-tuple-element.32), calls=%async_computation.10 | async-start | bytes 131072 | tf_op jit(solution)/shard_map/all_to_all | solution.py:266
  411.0 39.6 %all-to-all-start.11 = ((bf16[64,88,256]{2,1,0:T(8,128)(2,1)}), bf16[64,88,256]{2,1,0:T(8,128)(2,1)S(1)}, u32[]{:S(2)}, u32[]{:S(2)}) async-start(bf16[64,88,256]{2,1,0:T(8,128)(2,1)} %copy-done), calls=%async_computation.11 | async-start | bytes 5767168 | tf_op jit(solution)/shard_map/all_to_all | solution.py:266
  451.2 14.9 %collective-permute-start.18 = (bf16[88,256]{1,0:T(8,128)(2,1)S(1)}, bf16[88,256]{1,0:T(8,128)(2,1)S(1)}, u32[]{:S(2)}, u32[]{:S(2)}) collective-permute-start(bf16[88,256]{1,0:T(8,128)(2,1)S(1)} %get-tuple-element.45), channel_id=1, source_target_pairs={{0,0},{1,64},{2,32},{3,96},{4,1},{5,65},{6,33},{7,97},{8,2},{9,66}... | collective-permute-start | bytes 135176 | tf_op jit(solution)/shard_map/ppermute | solution.py:330
  460.2 9.8 %collective-permute-start.21 = (bf16[88,256]{1,0:T(8,128)(2,1)S(1)}, bf16[88,256]{1,0:T(8,128)(2,1)S(1)}, u32[]{:S(2)}, u32[]{:S(2)}) collective-permute-start(bf16[88,256]{1,0:T(8,128)(2,1)S(1)} %get-tuple-element.46), channel_id=1, source_target_pairs={{0,96},{1,32},{2,0},{3,64},{4,97},{5,33},{6,1},{7,65},{8,98},{9,34... | collective-permute-start | bytes 135176 | tf_op jit(solution)/shard_map/ppermute | solution.py:330
  462.3 9.6 %collective-permute-start.20 = (bf16[88,256]{1,0:T(8,128)(2,1)S(1)}, bf16[88,256]{1,0:T(8,128)(2,1)S(1)}, u32[]{:S(2)}, u32[]{:S(2)}) collective-permute-start(bf16[88,256]{1,0:T(8,128)(2,1)S(1)} %get-tuple-element.47), channel_id=1, source_target_pairs={{0,64},{1,0},{2,96},{3,32},{4,65},{5,1},{6,97},{7,33},{8,66},{9,2}... | collective-permute-start | bytes 135176 | tf_op jit(solution)/shard_map/ppermute | solution.py:330
  463.9 9.4 %collective-permute-start.19 = (bf16[88,256]{1,0:T(8,128)(2,1)S(1)}, bf16[88,256]{1,0:T(8,128)(2,1)S(1)}, u32[]{:S(2)}, u32[]{:S(2)}) collective-permute-start(bf16[88,256]{1,0:T(8,128)(2,1)S(1)} %get-tuple-element.48), channel_id=1, source_target_pairs={{0,32},{1,96},{2,64},{3,0},{4,33},{5,97},{6,65},{7,1},{8,34},{9,98... | collective-permute-start | bytes 135176 | tf_op jit(solution)/shard_map/ppermute | solution.py:330
  (17 other events, 119.4 us)
